TPU v7x, 128 devices: a whole 4x4x4 slice. The times are simulated.
128 devices in a mesh: dp: 16 (over x, y_lo, core), tensor: 8 (over z, y_hi).
Axes of the slice: x: 4, y: 4 (y_hi: 2, y_lo: 2; y = y_hi * 2 + y_lo), z: 4, core: 2. Of those that a mesh axis runs over, the one named last changes fastest.
Arguments:
- gate_pre: bfloat16 [6144, 14336], P('dp', 'tensor'), may hold values from -6 to 6
- up_pre: bfloat16 [6144, 14336], P('dp', 'tensor'), may hold values from -6 to 6
- out_grad: bfloat16 [6144, 4096], P('dp'), may hold values from -6 to 6
- old_weight: float32 [14336, 4096], P(('dp', 'tensor')), may hold values from -0.046875 to 0.046875
- old_first: float32 [14336, 4096], P(('dp', 'tensor')), may hold values from -8 to 8
- old_second: float32 [14336, 4096], P(('dp', 'tensor')), may hold values from 1 to 1000
Outputs:
- new_weight: float32 [14336, 4096], P('tensor', 'dp')
- new_first: float32 [14336, 4096], P('tensor', 'dp')
- new_second: float32 [14336, 4096], P('tensor', 'dp')
- grad_gate: bfloat16 [6144, 14336], P('dp', 'tensor')
- grad_up: bfloat16 [6144, 14336], P('dp', 'tensor')
All inputs are finite; a program needn't handle non-finite values.
Results may differ from a plain program's by a relative error of at most 0.0051.
Values may be sent and summed in bfloat16 or wider, within the bound.
A program may use at most 256 MiB of HBM per device.

v0:
```python
import jax
import jax.numpy as jnp
from jax import lax
from jax.sharding import PartitionSpec as P

beta_one = 0.9
beta_two = 0.95
learn_rate = 0.0003
decay_rate = 0.1
epsilon = 1e-08
step_count = 1001


def adamw(weight, first, second, grad):
    first_new = beta_one * first + (1.0 - beta_one) * grad
    second_new = beta_two * second + (1.0 - beta_two) * grad * grad
    first_hat = first_new / (1.0 - beta_one**step_count)
    second_hat = second_new / (1.0 - beta_two**step_count)
    weight_new = weight - learn_rate * (
        first_hat / (jnp.sqrt(second_hat) + epsilon) + decay_rate * weight
    )
    return (weight_new, first_new, second_new)


def retile(moved, dp_count, tensor_count):
    row_total = moved.shape[0]
    col_count = moved.shape[1]
    block_rows = row_total // dp_count
    shaped = moved.reshape(tensor_count, dp_count // tensor_count, block_rows, col_count)
    return jnp.transpose(shaped, (1, 0, 2, 3)).reshape(row_total, col_count)


def body(gate_pre, up_pre, out_grad, old_weight, old_first, old_second):
    dp_count = lax.axis_size("dp")
    tensor_count = lax.axis_size("tensor")
    moved = (
        lax.all_to_all(
            lax.all_to_all(old_weight, "dp", split_axis=1, concat_axis=0, tiled=True),
            "tensor",
            split_axis=0,
            concat_axis=0,
            tiled=True,
        ),
        lax.all_to_all(
            lax.all_to_all(old_first, "dp", split_axis=1, concat_axis=0, tiled=True),
            "tensor",
            split_axis=0,
            concat_axis=0,
            tiled=True,
        ),
        lax.all_to_all(
            lax.all_to_all(old_second, "dp", split_axis=1, concat_axis=0, tiled=True),
            "tensor",
            split_axis=0,
            concat_axis=0,
            tiled=True,
        ),
    )
    weight_tile = retile(moved[0], dp_count, tensor_count)
    first_tile = retile(moved[1], dp_count, tensor_count)
    second_tile = retile(moved[2], dp_count, tensor_count)
    gate_f = gate_pre.astype(jnp.float32)
    up_f = up_pre.astype(jnp.float32)
    sig = jax.nn.sigmoid(gate_f)
    hidden = (gate_f * sig * up_f).astype(jnp.bfloat16)
    weight_half = weight_tile.astype(jnp.bfloat16)
    hidden_grad = lax.dot_general(
        out_grad,
        lax.all_gather(weight_half, "dp", axis=1, tiled=True),
        (((1,), (1,)), ((), ())),
        preferred_element_type=jnp.float32,
    )
    grad_gate = (hidden_grad * up_f * sig * (1.0 + gate_f * (1.0 - sig))).astype(jnp.bfloat16)
    grad_up = (hidden_grad * gate_f * sig).astype(jnp.bfloat16)
    partial_grad = lax.dot_general(
        hidden, out_grad, (((0,), (0,)), ((), ())), preferred_element_type=jnp.float32
    )
    rounded = lax.optimization_barrier(partial_grad.astype(jnp.bfloat16)).astype(jnp.float32)
    weight_grad = lax.psum_scatter(rounded, "dp", scatter_dimension=1, tiled=True)
    new_weight, new_first, new_second = adamw(weight_tile, first_tile, second_tile, weight_grad)
    return (new_weight, new_first, new_second, grad_gate, grad_up)


def solution(mesh):
    placed = (
        P("dp", "tensor"),
        P("dp", "tensor"),
        P("dp", None),
        P(("dp", "tensor"), None),
        P(("dp", "tensor"), None),
        P(("dp", "tensor"), None),
    )
    return jax.shard_map(
        body,
        mesh=mesh,
        in_specs=placed,
        out_specs=(
            P("tensor", "dp"),
            P("tensor", "dp"),
            P("tensor", "dp"),
            P("dp", "tensor"),
            P("dp", "tensor"),
        ),
        check_vma=False,
    )
```

profile of v0, /device:TPU:1, one launch (start us, length us, event | category | flops | bytes accessed | tf_op | source)
XLA Modules:
  0.0 553.6 jit_solution(17537625235650375482)
XLA Ops:
  7.2 0.0 copy-start
  7.2 0.0 all-gather.2.cloned.1.call-start
  7.2 1.8 copy.34
  9.1 30.9 %all_to_all.75 = f32[112,16,256]{2,0,1:T(8,128)S(1)} all-to-all(f32[112,16,256]{2,0,1:T(8,128)S(1)} %bitcast.56), channel_id=1, replica_groups=mesh['dp'=16,'tensor'=8] {'dp'}, dimensions={1} | all-to-all | bytes 3670016 | tf_op jit(solution)/shard_map/all_to_all | solution.py:38
  39.9 31.9 %all_to_all.76 = f32[8,224,256]{2,1,0:T(8,128)S(1)} all-to-all(f32[8,224,256]{2,1,0:T(8,128)S(1)} %bitcast.52), channel_id=1, replica_groups=mesh['dp'=16,'tensor'=8] {'tensor'}, dimensions={0} | all-to-all | bytes 3670016 | tf_op jit(solution)/shard_map/all_to_all | solution.py:37
  71.8 0.1 copy.21
  72.0 0.0 copy-start.1
  72.0 1.2 copy-done.1
  73.2 1.0 bitcast_convert_fusion
  74.2 0.0 all-gather.2.cloned.1.call-update
  74.2 0.0 reduce-scatter.2.cloned.1.call-start
  74.3 0.0 copy-done
  74.3 10.2 %convolution_convert_fusion = bf16[1792,4096]{1,0:T(8,128)(2,1)S(1)} fusion(bf16[384,4096]{1,0:T(8,128)(2,1)S(1)} %copy-done, bf16[384,1792]{1,0:T(8,128)(2,1)} %param.7, bf16[384,1792]{1,0:T(8,128)(2,1)} %param.6), kind=kOutput, calls=%fused_computation | convolution fusion | flops 5649989632 | bytes 20578304 | tf_op jit(solution)/shard_map/dot_general | solution.py:75
  84.5 10.2 %convert_element_type.28 = f32[1792,4096]{1,0:T(8,128)} convert(bf16[1792,4096]{1,0:T(8,128)(2,1)S(1)} %convolution_convert_fusion) | non-fusion elementwise | flops 7340032 | bytes 44040192 | tf_op jit(solution)/shard_map/convert_element_type | solution.py:78
  94.7 0.0 reduce-scatter.2.cloned.1.call-update
  94.7 3.0 copy.33
  97.6 6.0 %all-to-all-start.2 = ((f32[112,16,256]{2,0,1:T(8,128)}), f32[112,16,256]{2,0,1:T(8,128)}, u32[]{:S(2)}, u32[]{:S(2)}) async-start(f32[112,16,256]{2,0,1:T(8,128)} %bitcast.50), calls=%async_computation.2 | async-start | bytes 3670016 | tf_op jit(solution)/shard_map/all_to_all | solution.py:45
  103.6 2.9 copy.32
  106.5 28.9 %all-to-all-done.2 = f32[112,16,256]{2,0,1:T(8,128)} async-done(((f32[112,16,256]{2,0,1:T(8,128)}), f32[112,16,256]{2,0,1:T(8,128)}, u32[]{:S(2)}, u32[]{:S(2)}) %all-to-all-start.2) | async-done | bytes 1835040 | tf_op jit(solution)/shard_map/all_to_all | solution.py:45
  135.4 43.3 %all_to_all.77 = f32[112,16,256]{2,0,1:T(8,128)} all-to-all(f32[112,16,256]{2,0,1:T(8,128)} %bitcast.51), channel_id=1, replica_groups=mesh['dp'=16,'tensor'=8] {'dp'}, dimensions={1} | all-to-all | bytes 3670016 | tf_op jit(solution)/shard_map/all_to_all | solution.py:52
  178.8 42.6 %all_to_all.78 = f32[8,224,256]{2,1,0:T(8,128)} all-to-all(f32[8,224,256]{2,1,0:T(8,128)} %bitcast.6), channel_id=1, replica_groups=mesh['dp'=16,'tensor'=8] {'tensor'}, dimensions={0} | all-to-all | bytes 3670016 | tf_op jit(solution)/shard_map/all_to_all | solution.py:44
  221.4 4.5 all-to-all-start.5
  225.9 1.7 broadcast_multiply_fusion.1
  227.6 1.3 copy.23
  228.9 69.2 %all-to-all-done.5 = f32[8,224,256]{2,1,0:T(8,128)} async-done(((f32[8,224,256]{2,1,0:T(8,128)}), f32[8,224,256]{2,1,0:T(8,128)}, u32[]{:S(2)}, u32[]{:S(2)}) %all-to-all-start.5) | async-done | bytes 1835040 | tf_op jit(solution)/shard_map/all_to_all | solution.py:51
  298.1 1.8 broadcast_multiply_fusion
  299.9 1.3 copy.25
  301.2 0.0 all-gather.2.cloned.1.call-done
  301.2 17.5 %fusion.9 = (bf16[384,1792]{1,0:T(8,128)(2,1)}, bf16[384,1792]{1,0:T(8,128)(2,1)}) fusion(bf16[384,1792]{1,0:T(8,128)(2,1)} %param.6, bf16[384,1792]{1,0:T(8,128)(2,1)} %param.7, bf16[384,4096]{1,0:T(8,128)(2,1)S(1)} %copy-done, bf16[1792,4096]{1,0:T(8,128)(2,1)} %all-gather.2.cloned.1.call-done), kind=kOutput, calls=%fused_computation.16 | convolution fusion | flops 5647466496 | bytes 23330816 | tf_op jit(solution)/shard_map/dot_general | solution.py:67
  318.7 221.9 %reduce-scatter.2.cloned.1.call-done = f32[1792,256]{1,0:T(8,128)} async-done(((f32[1792,4096]{1,0:T(8,128)}), f32[1792,256]{1,0:T(8,128)}) %reduce-scatter.2.cloned.1.call-update) | async-done | bytes 1835024 | tf_op jit(solution)/shard_map/reduce_scatter | solution.py:79
  540.6 6.2 %bitcast_subtract_fusion = (f32[1792,256]{1,0:T(8,128)}, f32[1792,256]{1,0:T(8,128)}, f32[1792,256]{1,0:T(8,128)}) fusion(f32[2,8,112,256]{3,2,1,0:T(8,128)} %copy-done.1, f32[1792,256]{1,0:T(8,128)} %reduce-scatter.2.cloned.1.call-done, f32[2,8,112,256]{3,2,1,0:T(8,128)} %copy.25, f32[2,8,112,256]{3,2,1,0:T(8,128)} %copy.23), kind=kLoop, calls=%fused_computation.24 | loop fusion | flops 5046272 | bytes 12845056 | tf_op jit(solution)/shard_map/sub | solution.py:19
Async XLA Ops:
  7.2 67.1 %copy-start = (bf16[384,4096]{1,0:T(8,128)(2,1)S(1)}, bf16[384,4096]{1,0:T(8,128)(2,1)}, u32[]{:S(2)}) copy-start(bf16[384,4096]{1,0:T(8,128)(2,1)} %param.8) | copy-start | bytes 9437188
  7.2 294.1 %all-gather.2.cloned.1.call-start = ((), (), s32[]{:S(2)}) async-start(), calls=%async_computation.8 | async-start | bytes 15597568 | tf_op jit(solution)/shard_map/all_gather | solution.py:69
  72.0 1.2 copy-start.1
  74.2 466.4 %reduce-scatter.2.cloned.1.call-start = ((), (), s32[]{:S(2)}) async-start(), calls=%async_computation.7 | async-start | bytes 31195136 | tf_op jit(solution)/shard_map/reduce_scatter | solution.py:79
  97.6 37.8 %all-to-all-start.2 = ((f32[112,16,256]{2,0,1:T(8,128)}), f32[112,16,256]{2,0,1:T(8,128)}, u32[]{:S(2)}, u32[]{:S(2)}) async-start(f32[112,16,256]{2,0,1:T(8,128)} %bitcast.50), calls=%async_computation.2 | async-start | bytes 3670016 | tf_op jit(solution)/shard_map/all_to_all | solution.py:45
  221.4 76.8 %all-to-all-start.5 = ((f32[8,224,256]{2,1,0:T(8,128)}), f32[8,224,256]{2,1,0:T(8,128)}, u32[]{:S(2)}, u32[]{:S(2)}) async-start(f32[8,224,256]{2,1,0:T(8,128)} %bitcast.49), calls=%async_computation.6 | async-start | bytes 3670016 | tf_op jit(solution)/shard_map/all_to_all | solution.py:51
Sparse Core Ops, SparseCore 0:
  74.4 135.3 all-gather.1
  212.1 328.4 reduce-scatter.1
where the time goes:
time: 554 us
  waiting for transfers between devices  320 us (58%)
  blocking collectives  149 us (27%)
  matrix products  27.7 us (5%)
  other arithmetic  20.7 us (4%)
  between operations  14.1 us (3%)
  local copies, waits for them, and re-layouts  11.8 us (2%)
  starting transfers between devices  10.6 us (2%)
    reduce_scatter x1, waiting for transfers between devices, body(): lax.psum_scatter(rounded, 'dp', scatter_dimension=1, tiled=True)  222 us
    all_to_all x1, waiting for transfers between devices, body(): lax.all_to_all(lax.all_to_all(old_second, 'dp', split_axis=1, concat_axis...  69.2 us
    all_to_all x1, blocking collectives, body(): lax.all_to_all(old_second, 'dp', split_axis=1, concat_axis=0, tiled=True)  43.3 us
    all_to_all x1, blocking collectives, body(): lax.all_to_all(lax.all_to_all(old_first, 'dp', split_axis=1, concat_axis=...  42.6 us
    all_to_all x1, blocking collectives, body(): lax.all_to_all(lax.all_to_all(old_weight, 'dp', split_axis=1, concat_axis...  31.9 us
    all_to_all x1, blocking collectives, body(): lax.all_to_all(old_weight, 'dp', split_axis=1, concat_axis=0, tiled=True)  30.9 us
    all_to_all x1, waiting for transfers between devices, body(): lax.all_to_all(old_first, 'dp', split_axis=1, concat_axis=0, tiled=True)  28.9 us
    dot_general x1, matrix products, body(): lax.dot_general(out_grad, lax.all_gather(weight_half, 'dp', axis=1, tiled...  17.5 us
  transfers between devices with their start and end apart: 4, of which 3 were waited for; matrix products, arithmetic and copies ran while one was open for 9% of the time, Pallas kernels for 0%

commit v1 on v0

v1 whole, which is shorter than its diff:
```python
import functools
import jax
import jax.numpy as jnp
from jax import lax
from jax.experimental import pallas as pl
from jax.experimental.pallas import tpu as pltpu
from jax.sharding import PartitionSpec as P

beta_one = 0.9
beta_two = 0.95
learn_rate = 0.0003
decay_rate = 0.1
epsilon = 1e-08
step_count = 1001

MESH = pl.DeviceIdType.MESH
BF16 = jnp.bfloat16
F32 = jnp.float32


def adamw(weight, first, second, grad):
    first_new = beta_one * first + (1.0 - beta_one) * grad
    second_new = beta_two * second + (1.0 - beta_two) * grad * grad
    first_hat = first_new / (1.0 - beta_one**step_count)
    second_hat = second_new / (1.0 - beta_two**step_count)
    weight_new = weight - learn_rate * (
        first_hat / (jnp.sqrt(second_hat) + epsilon) + decay_rate * weight
    )
    return (weight_new, first_new, second_new)


def device(x, yl, c, z, yh):
    return ((x * 2 + yl) * 2 + c, z * 2 + yh)


def kernel(
    gate_hbm, up_hbm, og_hbm, w_hbm, m_hbm, v_hbm,
    gg_hbm, gu_hbm, grad_out, mv_out, wt_out,
    gate, up, w32, m32, v32, wb, mvb, og_all, h_own, h_all, w_all,
    part, rs, summed, hg, hg_all, gg, gu,
    load_sem, store_sem,
    ogy_s, ogy_r, ogz_s, ogz_r, ogc_s, ogc_r, h_s, h_r, w_s, w_r, mv_s, mv_r,
    hg_s, hg_r, wt_s, wt_r, rs_s, rs_r, g_s, g_r,
):
    d = lax.axis_index("dp")
    q = lax.axis_index("tensor")
    p = d // 2
    c = lax.rem(d, 2)
    x = p // 2
    yl = lax.rem(p, 2)
    z = q // 2
    yh = lax.rem(q, 2)
    tok, ff = gate.shape
    blk = w32.shape[0]
    cols = w32.shape[1]
    sub = cols // 16
    rows = 4 * blk
    tq = tok // 4
    mine = 2 * c + yl
    diag = p == q
    diag_i = jnp.where(diag, 1, 0)

    def mult(v, n):
        return pl.multiple_of(v, n)

    def peer(r):
        pyl = lax.rem(yl + r % 2, 2)
        pc = lax.rem(c + r // 2, 2)
        return device(x, pyl, pc, z, yh), 2 * pc + pyl, 2 * pyl + pc

    def across(r):
        return lax.rem(x + r, 4)

    loads = [
        pltpu.make_async_copy(og_hbm, og_all.at[pl.ds(mult(mine * tok, tok), tok)], load_sem.at[0]),
        pltpu.make_async_copy(w_hbm, w32, load_sem.at[1]),
        pltpu.make_async_copy(gate_hbm, gate, load_sem.at[2]),
        pltpu.make_async_copy(up_hbm, up, load_sem.at[3]),
        pltpu.make_async_copy(m_hbm, m32, load_sem.at[4]),
        pltpu.make_async_copy(v_hbm, v32, load_sem.at[5]),
    ]
    for load in loads:
        load.start()

    barrier = pltpu.get_barrier_semaphore()

    @pl.loop(0, 16)
    def _(n):
        @pl.when(jnp.logical_not(jnp.logical_and(diag, n == d)))
        def _():
            pl.semaphore_signal(barrier, inc=1, device_id=(n, p), device_id_type=MESH)

        sd = 2 * q + n // 8
        st = lax.rem(n, 8)

        @pl.when(jnp.logical_not(jnp.logical_and(sd == d, st == q)))
        def _():
            pl.semaphore_signal(barrier, inc=1, device_id=(sd, st), device_id_type=MESH)

    for r in range(1, 4):
        pl.semaphore_signal(barrier, inc=1, device_id=peer(r)[0], device_id_type=MESH)
        pl.semaphore_signal(
            barrier, inc=1, device_id=device(across(r), yl, c, z, yh), device_id_type=MESH
        )
        pl.semaphore_signal(
            barrier, inc=1, device_id=device(x, yl, c, lax.rem(z + r, 4), yh), device_id_type=MESH
        )

    loads[1].wait()
    wb[...] = w32[...].astype(BF16)
    loads[0].wait()
    pl.semaphore_wait(barrier, 41 - 2 * diag_i)

    def remote(src, dst, ss, rr, to):
        return pltpu.make_async_remote_copy(
            src_ref=src, dst_ref=dst, send_sem=ss, recv_sem=rr, device_id=to, device_id_type=MESH
        )

    sends = []

    def go(*args):
        copy = remote(*args)
        copy.start()
        sends.append(copy)

    def og_rows(slot, part_index):
        return og_all.at[pl.ds(mult(slot * tok + part_index * tq, tq), tq)]

    def og_slot(slot):
        return og_all.at[pl.ds(mult(slot * tok, tok), tok)]

    side, side_slot, _ = peer(1)
    core, core_slot, _ = peer(2)
    _, far_slot, _ = peer(3)
    go(og_rows(mine, z), og_rows(mine, z), ogy_s, ogy_r, side)
    go(og_slot(mine), og_slot(mine), ogc_s.at[4], ogc_r.at[4], core)

    block = 2 * lax.rem(z, 2) + yh
    w_dst = w_all.at[pl.ds(mult(block * blk, blk), blk)]
    w_yl = z // 2
    self_w = jnp.logical_and(diag, w_yl == yl)
    for r in range(1, 4):
        go(wb, w_dst, w_s.at[r], w_r.at[block], device(across(r), w_yl, c, x, yl))
    w_home = remote(wb, w_dst, w_s.at[0], w_r.at[block], device(x, w_yl, c, x, yl))

    @pl.when(self_w)
    def _():
        pltpu.make_async_copy(wb, w_dst, w_r.at[block]).start()

    @pl.when(jnp.logical_not(self_w))
    def _():
        w_home.start()

    loads[4].wait()
    loads[5].wait()
    for n in range(16):
        mvb[n, 0] = m32[:, n * sub : (n + 1) * sub].astype(BF16)
        mvb[n, 1] = v32[:, n * sub : (n + 1) * sub].astype(BF16)
    mv_dst = mv_out.at[:, pl.ds(mult((8 * c + q) * blk, blk), blk), :]

    @pl.when(diag)
    def _():
        pltpu.make_async_copy(mvb.at[d], mv_dst, mv_r).start()

    @pl.when(jnp.logical_not(diag))
    def _():
        remote(mvb.at[d], mv_dst, mv_s.at[0], mv_r, (d, p)).start()

    @pl.loop(1, 16)
    def _(r):
        n = lax.rem(d + r, 16)
        remote(mvb.at[n], mv_dst, mv_s.at[r], mv_r, (n, p)).start()

    loads[2].wait()
    loads[3].wait()

    @pl.loop(0, ff // 128)
    def _(b):
        at = pl.ds(mult(b * 128, 128), 128)
        g = gate[:, at].astype(F32)
        u = up[:, at].astype(F32)
        h = g * jax.nn.sigmoid(g) * u
        h_own[at, :] = h.T.astype(BF16)

    my_cols = pl.ds(mult(mine * tok, 128), tok)
    for r in range(1, 4):
        to, slot, _ = peer(r)
        go(h_own.at[pl.ds(mult(slot * rows, rows), rows)], h_all.at[:, my_cols],
           h_s.at[r - 1], h_r.at[r - 1], to)
    h_all[:, my_cols] = h_own[pl.ds(mult(mine * rows, rows), rows), :]

    got = og_rows(side_slot, z)
    remote(got, got, ogy_s, ogy_r, side).wait_recv()
    for r in range(1, 4):
        go(got, got, ogz_s.at[r - 1], ogz_r.at[r - 1], device(x, yl, c, lax.rem(z + r, 4), yh))
    go(got, got, ogc_s.at[0], ogc_r.at[0], core)
    for r in (1, 3, 2):
        got = og_rows(side_slot, lax.rem(z + 4 - r, 4))
        remote(got, got, ogz_s.at[r - 1], ogz_r.at[r - 1], side).wait_recv()
        go(got, got, ogc_s.at[r], ogc_r.at[r], core)

    for r in range(1, 4):
        _, slot, _ = peer(r)
        there = h_all.at[:, pl.ds(mult(slot * tok, 128), tok)]
        remote(there, there, h_s.at[r - 1], h_r.at[r - 1], side).wait_recv()
    remote(og_slot(core_slot), og_slot(core_slot), ogc_s.at[4], ogc_r.at[4], core).wait_recv()
    for r in range(4):
        got = og_rows(far_slot, lax.rem(z + 4 - r, 4))
        remote(got, got, ogc_s.at[r], ogc_r.at[r], core).wait_recv()

    @pl.loop(0, 4)
    def _(k):
        for r in (1, 3, 2, 0):
            to_x = across(r)
            at = pl.ds(mult((to_x * 4 + k) * sub, 128), sub)
            part[r, k] = jnp.dot(
                h_all[...], og_all[:, at], preferred_element_type=F32
            ).astype(BF16)
            if r:
                remote(part.at[r, k], rs.at[r - 1, k], rs_s.at[r - 1, k], rs_r.at[r - 1, k],
                       device(to_x, yl, c, z, yh)).start()

    for i in range(4):
        there = w_all.at[pl.ds(i * blk, blk)]
        remote(there, there, w_s.at[0], w_r.at[i], side).wait_recv()
    my_rows = pl.ds(mult(mine * rows, rows), rows)
    for r in range(1, 4):
        to, _, k = peer(r)
        go(w_all.at[:, pl.ds(mult((x * 4 + k) * sub, 128), sub)], wt_out.at[my_rows],
           wt_s.at[r - 1], wt_r.at[r - 1], to)
    wt_own = pltpu.make_async_copy(
        w_all.at[:, pl.ds(mult(d * sub, 128), sub)], wt_out.at[my_rows], store_sem.at[0]
    )
    wt_own.start()

    n_tile = 4 * tok // 6

    @pl.loop(0, 6)
    def _(n):
        at = pl.ds(mult(n * n_tile, n_tile), n_tile)
        hg[:, at] = lax.dot_general(
            w_all[...], og_all[at, :], (((1,), (1,)), ((), ())), preferred_element_type=F32
        ).astype(BF16)

    for r in range(1, 4):
        to, slot, _ = peer(r)
        go(hg.at[:, pl.ds(mult(slot * tok, 128), tok)], hg_all.at[my_rows],
           hg_s.at[r - 1], hg_r.at[r - 1], to)
    hg_all[my_rows, :] = hg[:, my_cols]

    def reduce_chunk(k):
        for r in range(3):
            remote(rs.at[r, k], rs.at[r, k], rs_s.at[r, k], rs_r.at[r, k], side).wait_recv()
        summed[k] = (
            part[0, k].astype(F32) + rs[0, k].astype(F32)
            + (rs[1, k].astype(F32) + rs[2, k].astype(F32))
        ).astype(BF16)
        k_yl = k // 2
        k_c = k % 2
        r = (1 - jnp.where(k_yl == yl, 1, 0)) + 2 * (1 - jnp.where(k_c == c, 1, 0))
        local = r == 0
        dst = grad_out.at[my_rows]

        @pl.when(local)
        def _():
            pltpu.make_async_copy(summed.at[k], dst, store_sem.at[1]).start()

        @pl.when(jnp.logical_not(local))
        def _():
            remote(summed.at[k], dst, g_s.at[r], g_r.at[r], device(x, k_yl, k_c, z, yh)).start()

    def finish_grads():
        for r in range(1, 4):
            _, slot, _ = peer(r)
            there = hg_all.at[pl.ds(mult(slot * rows, rows), rows)]
            remote(there, there, hg_s.at[r - 1], hg_r.at[r - 1], side).wait_recv()

        @pl.loop(0, ff // 128)
        def _(b):
            at = pl.ds(mult(b * 128, 128), 128)
            back = hg_all[at, :].astype(F32).T
            g = gate[:, at].astype(F32)
            u = up[:, at].astype(F32)
            s = jax.nn.sigmoid(g)
            gg[:, at] = (back * u * s * (1.0 + g * (1.0 - s))).astype(BF16)
            gu[:, at] = (back * g * s).astype(BF16)

        pltpu.make_async_copy(gg, gg_hbm, store_sem.at[2]).start()
        pltpu.make_async_copy(gu, gu_hbm, store_sem.at[3]).start()

    for k in range(4):
        if k == 3:
            finish_grads()
        reduce_chunk(k)

    for copy in sends:
        copy.wait_send()

    @pl.when(jnp.logical_not(self_w))
    def _():
        w_home.wait_send()

    @pl.when(jnp.logical_not(diag))
    def _():
        remote(mvb.at[0], mv_dst, mv_s.at[0], mv_r, side).wait_send()

    for r in range(1, 16):
        remote(mvb.at[r], mv_dst, mv_s.at[r], mv_r, side).wait_send()
    for r in range(3):
        for k in range(4):
            remote(part.at[r + 1, k], rs.at[r, k], rs_s.at[r, k], rs_r.at[r, k], side).wait_send()
    pltpu.make_async_copy(gg, gg_hbm, store_sem.at[2]).wait()
    pltpu.make_async_copy(gu, gu_hbm, store_sem.at[3]).wait()
    wt_own.wait()
    pltpu.make_async_copy(summed.at[0], grad_out.at[my_rows], store_sem.at[1]).wait()
    for r in range(1, 4):
        _, slot, _ = peer(r)
        there = pl.ds(mult(slot * rows, rows), rows)
        remote(wt_out.at[there], wt_out.at[there], wt_s.at[r - 1], wt_r.at[r - 1], side).wait_recv()
        remote(summed.at[r], grad_out.at[there], g_s.at[r], g_r.at[r], side).wait()
    remote(mv_out, mv_out, mv_s.at[0], mv_r, side).wait_recv()


def body(gate_pre, up_pre, out_grad, old_weight, old_first, old_second):
    tok, ff = gate_pre.shape
    blk, cols = old_weight.shape
    rows = 4 * blk
    sub = cols // 16
    anyspec = pl.BlockSpec(memory_space=pl.ANY)
    dma = pltpu.SemaphoreType.DMA
    gg, gu, grad, moments, weight = pl.pallas_call(
        kernel,
        out_shape=(
            jax.ShapeDtypeStruct((tok, ff), BF16),
            jax.ShapeDtypeStruct((tok, ff), BF16),
            jax.ShapeDtypeStruct((ff, sub), BF16),
            jax.ShapeDtypeStruct((2, ff, sub), BF16),
            jax.ShapeDtypeStruct((ff, sub), BF16),
        ),
        in_specs=[anyspec] * 6,
        out_specs=(anyspec,) * 5,
        scratch_shapes=[
            pltpu.VMEM((tok, ff), BF16),
            pltpu.VMEM((tok, ff), BF16),
            pltpu.VMEM((blk, cols), F32),
            pltpu.VMEM((blk, cols), F32),
            pltpu.VMEM((blk, cols), F32),
            pltpu.VMEM((blk, cols), BF16),
            pltpu.VMEM((16, 2, blk, sub), BF16),
            pltpu.VMEM((4 * tok, cols), BF16),
            pltpu.VMEM((ff, tok), BF16),
            pltpu.VMEM((rows, 4 * tok), BF16),
            pltpu.VMEM((rows, cols), BF16),
            pltpu.VMEM((4, 4, rows, sub), BF16),
            pltpu.VMEM((3, 4, rows, sub), BF16),
            pltpu.VMEM((4, rows, sub), BF16),
            pltpu.VMEM((rows, 4 * tok), BF16),
            pltpu.VMEM((ff, tok), BF16),
            pltpu.VMEM((tok, ff), BF16),
            pltpu.VMEM((tok, ff), BF16),
            dma((6,)),
            dma((4,)),
            dma(()), dma(()),
            dma((3,)), dma((3,)),
            dma((5,)), dma((5,)),
            dma((3,)), dma((3,)),
            dma((4,)), dma((4,)),
            dma((16,)), dma(()),
            dma((3,)), dma((3,)),
            dma((3,)), dma((3,)),
            dma((3, 4)), dma((3, 4)),
            dma((4,)), dma((4,)),
        ],
        compiler_params=pltpu.CompilerParams(
            collective_id=0, has_side_effects=True, vmem_limit_bytes=60 << 20
        ),
        cost_estimate=pl.CostEstimate(
            flops=4 * tok * ff * cols, bytes_accessed=6 * tok * ff * 2, transcendentals=2 * tok * ff
        ),
        name="step",
    )(gate_pre, up_pre, out_grad, old_weight, old_first, old_second)
    new_weight, new_first, new_second = adamw(
        weight.astype(F32), moments[0].astype(F32), moments[1].astype(F32), grad.astype(F32)
    )
    return (new_weight, new_first, new_second, gg, gu)


def solution(mesh):
    placed = (
        P("dp", "tensor"),
        P("dp", "tensor"),
        P("dp", None),
        P(("dp", "tensor"), None),
        P(("dp", "tensor"), None),
        P(("dp", "tensor"), None),
    )
    return jax.shard_map(
        body,
        mesh=mesh,
        in_specs=placed,
        out_specs=(
            P("tensor", "dp"),
            P("tensor", "dp"),
            P("tensor", "dp"),
            P("dp", "tensor"),
            P("dp", "tensor"),
        ),
        check_vma=False,
    )
```

time: 554 us -> 270 us (0.49)
  the two profiles are of different devices: /device:TPU:1 before, /device:TPU:7 now
where the time goes in v1:
time: 270 us
  Pallas kernels  261 us (97%)
  other arithmetic  5.46 us (2%)
  local copies, waits for them, and re-layouts  2.91 us (1%)
    pallas_call x1, Pallas kernels, body(): pl.pallas_call(kernel, out_shape=(jax.ShapeDtypeStruct((tok, ff), BF16),...  261 us
    sub x1, other arithmetic, adamw(): weight - learn_rate * (first_hat / (jnp.sqrt(second_hat) + epsilon) + dec...  5.46 us

profile of v1, /device:TPU:7, one launch (start us, length us, event | category | flops | bytes accessed | tf_op | source)
XLA Modules:
  0.0 269.7 jit_solution(4047954027768077039)
XLA Ops:
  0.6 260.7 %step.1 = (bf16[384,1792]{1,0:T(8,128)(2,1)}, bf16[384,1792]{1,0:T(8,128)(2,1)}, bf16[1792,256]{1,0:T(8,128)(2,1)}, bf16[2,1792,256]{2,1,0:T(8,128)(2,1)}, bf16[1792,256]{1,0:T(8,128)(2,1)}) custom-call(bf16[384,1792]{1,0:T(8,128)(2,1)} %gate_hbm.1, bf16[384,1792]{1,0:T(8,128)(2,1)} %up_hbm.1, bf16[384,4096]{1,0:T(8,128)(2,1)} %og_hbm.1, f32[112,4096]{1,0:T(8,128)} %w_hbm.1, ...), custom_call_target="tpu_custom_call" | custom-call | flops 11274289152 | bytes 8257536 | tf_op jit(solution)/shard_map/step/pallas_call | solution.py:331
  261.4 0.0 copy-start.1
  261.4 5.5 %convert_subtract_fusion = (f32[1792,256]{1,0:T(8,128)}, f32[1792,256]{1,0:T(8,128)}, f32[1792,256]{1,0:T(8,128)}) fusion(bf16[1792,256]{1,0:T(8,128)(2,1)} %get-tuple-element.10, bf16[1792,256]{1,0:T(8,128)(2,1)} %get-tuple-element.12, bf16[2,1792,256]{2,1,0:T(8,128)(2,1)} %get-tuple-element.11), kind=kLoop, calls=%fused_computation.2 | loop fusion | flops 7798784 | bytes 9175040 | tf_op jit(solution)/shard_map/sub | solution.py:26
  266.8 0.0 copy-start
  266.8 0.0 copy-done.1
  266.8 1.1 copy.13
  267.9 0.8 copy-done
  268.7 1.1 copy.14
Async XLA Ops:
  261.4 5.5 %copy-start.1 = (bf16[384,1792]{1,0:T(8,128)(2,1)S(1)}, bf16[384,1792]{1,0:T(8,128)(2,1)}, u32[]{:S(2)}) copy-start(bf16[384,1792]{1,0:T(8,128)(2,1)} %get-tuple-element.26) | copy-start | bytes 4128772
  266.8 1.8 copy-start

commit v2 on v1

--- a/solution.py
+++ b/solution.py
@@ -39,7 +39,7 @@
     gate, up, w32, m32, v32, wb, mvb, og_all, h_own, h_all, w_all,
     part, rs, summed, hg, hg_all, gg, gu,
     load_sem, store_sem,
-    ogy_s, ogy_r, ogz_s, ogz_r, ogc_s, ogc_r, h_s, h_r, w_s, w_r, mv_s, mv_r,
+    ogy_s, ogy_r, ogz_s, ogz_r, ogc_s, ogc_r, h_s, h_r, w_s, w_r, wx_s, wx_r, mv_s, mv_r,
     hg_s, hg_r, wt_s, wt_r, rs_s, rs_r, g_s, g_r,
 ):
     d = lax.axis_index("dp")
@@ -106,9 +106,10 @@
             barrier, inc=1, device_id=device(x, yl, c, lax.rem(z + r, 4), yh), device_id_type=MESH
         )
 
+    loads[0].wait()
     loads[1].wait()
-    wb[...] = w32[...].astype(BF16)
-    loads[0].wait()
+    for n in range(4):
+        wb[n] = w32[:, n * 4 * sub : (n + 1) * 4 * sub].astype(BF16)
     pl.semaphore_wait(barrier, 41 - 2 * diag_i)
 
     def remote(src, dst, ss, rr, to):
@@ -123,8 +124,11 @@
         copy.start()
         sends.append(copy)
 
-    def og_rows(slot, part_index):
-        return og_all.at[pl.ds(mult(slot * tok + part_index * tq, tq), tq)]
+    half = tq // 2
+
+    def og_half(slot, part_index, side_half):
+        start = mult(slot * tok + part_index * tq + side_half * half, half)
+        return og_all.at[pl.ds(start, half)]
 
     def og_slot(slot):
         return og_all.at[pl.ds(mult(slot * tok, tok), tok)]
@@ -132,24 +136,34 @@
     side, side_slot, _ = peer(1)
     core, core_slot, _ = peer(2)
     _, far_slot, _ = peer(3)
-    go(og_rows(mine, z), og_rows(mine, z), ogy_s, ogy_r, side)
-    go(og_slot(mine), og_slot(mine), ogc_s.at[4], ogc_r.at[4], core)
+    for i in range(2):
+        mine_half = og_half(mine, z, i)
+        go(mine_half, mine_half, ogy_s.at[i], ogy_r.at[i], side)
 
     block = 2 * lax.rem(z, 2) + yh
-    w_dst = w_all.at[pl.ds(mult(block * blk, blk), blk)]
     w_yl = z // 2
     self_w = jnp.logical_and(diag, w_yl == yl)
-    for r in range(1, 4):
-        go(wb, w_dst, w_s.at[r], w_r.at[block], device(across(r), w_yl, c, x, yl))
-    w_home = remote(wb, w_dst, w_s.at[0], w_r.at[block], device(x, w_yl, c, x, yl))
+
+    def w_cols(at_x):
+        return pl.ds(mult(at_x * 4 * sub, 128), 4 * sub)
+
+    def w_place(at_x):
+        return w_all.at[pl.ds(mult(block * blk, blk), blk), w_cols(at_x)]
+
+    for r in (1, 3, 2):
+        go(wb.at[across(r)], w_place(across(r)), w_s.at[r], w_r.at[block],
+           device(across(r), w_yl, c, x, yl))
+    w_home = remote(wb.at[x], w_place(x), w_s.at[0], w_r.at[block], device(x, w_yl, c, x, yl))
 
     @pl.when(self_w)
     def _():
-        pltpu.make_async_copy(wb, w_dst, w_r.at[block]).start()
+        pltpu.make_async_copy(wb.at[x], w_place(x), w_r.at[block]).start()
 
     @pl.when(jnp.logical_not(self_w))
     def _():
         w_home.start()
+
+    go(og_slot(mine), og_slot(mine), ogc_s.at[8], ogc_r.at[8], core)
 
     loads[4].wait()
     loads[5].wait()
@@ -189,24 +203,76 @@
            h_s.at[r - 1], h_r.at[r - 1], to)
     h_all[:, my_cols] = h_own[pl.ds(mult(mine * rows, rows), rows), :]
 
-    got = og_rows(side_slot, z)
-    remote(got, got, ogy_s, ogy_r, side).wait_recv()
-    for r in range(1, 4):
-        go(got, got, ogz_s.at[r - 1], ogz_r.at[r - 1], device(x, yl, c, lax.rem(z + r, 4), yh))
-    go(got, got, ogc_s.at[0], ogc_r.at[0], core)
-    for r in (1, 3, 2):
-        got = og_rows(side_slot, lax.rem(z + 4 - r, 4))
-        remote(got, got, ogz_s.at[r - 1], ogz_r.at[r - 1], side).wait_recv()
-        go(got, got, ogc_s.at[r], ogc_r.at[r], core)
+    z_next = device(x, yl, c, lax.rem(z + 1, 4), yh)
+    z_prev = device(x, yl, c, lax.rem(z + 3, 4), yh)
+    x_next = device(across(1), yl, c, z, yh)
+    x_prev = device(across(3), yl, c, z, yh)
+
+    def quarter(r):
+        return lax.rem(z + 4 - r, 4)
+
+    def z_piece(i):
+        return og_half(side_slot, quarter((1, 1, 3, 3, 2, 2)[i]), i % 2)
+
+    def z_wait(i):
+        got = z_piece(i)
+        remote(got, got, ogz_s.at[i], ogz_r.at[i], z_next).wait_recv()
+        if i == 0:
+            go(got, got, ogz_s.at[4], ogz_r.at[4], z_next)
+        if i == 3:
+            go(got, got, ogz_s.at[5], ogz_r.at[5], z_prev)
+        go(got, got, ogc_s.at[2 + i], ogc_r.at[2 + i], core)
+
+    def y_wait(i):
+        got = og_half(side_slot, z, i)
+        remote(got, got, ogy_s.at[i], ogy_r.at[i], side).wait_recv()
+        up_z = (got, got, ogz_s.at[i], ogz_r.at[i], z_next)
+        down_z = (got, got, ogz_s.at[2 + i], ogz_r.at[2 + i], z_prev)
+        for which in ((up_z, down_z), (down_z, up_z))[i]:
+            go(*which)
+        go(got, got, ogc_s.at[i], ogc_r.at[i], core)
+
+    half_rows = rows // 2
+
+    def w_half(at_x, i):
+        return w_all.at[pl.ds(i * half_rows, half_rows), w_cols(at_x)]
+
+    def wx_piece(i):
+        return w_half(across((3, 3, 1, 1, 2, 2)[i]), i % 2)
+
+    def wx_wait(i):
+        got = wx_piece(i)
+        remote(got, got, wx_s.at[i], wx_r.at[i], x_next).wait_recv()
+        if i == 0:
+            go(got, got, wx_s.at[4], wx_r.at[4], x_next)
+        if i == 3:
+            go(got, got, wx_s.at[5], wx_r.at[5], x_prev)
+
+    y_wait(0)
+    for i in range(4):
+        there = w_all.at[pl.ds(i * blk, blk), w_cols(x)]
+        remote(there, there, w_s.at[0], w_r.at[i], side).wait_recv()
+    for i in range(2):
+        got = w_half(x, i)
+        mate = w_half(x, 1 - i)
+        go(got, got, wx_s.at[i], wx_r.at[i], x_next)
+        go(mate, mate, wx_s.at[3 - i], wx_r.at[3 - i], x_prev)
+    y_wait(1)
+    z_wait(0)
+    z_wait(3)
+    wx_wait(0)
+    wx_wait(3)
+    for i in (1, 2, 4, 5):
+        z_wait(i)
 
     for r in range(1, 4):
         _, slot, _ = peer(r)
         there = h_all.at[:, pl.ds(mult(slot * tok, 128), tok)]
         remote(there, there, h_s.at[r - 1], h_r.at[r - 1], side).wait_recv()
-    remote(og_slot(core_slot), og_slot(core_slot), ogc_s.at[4], ogc_r.at[4], core).wait_recv()
-    for r in range(4):
-        got = og_rows(far_slot, lax.rem(z + 4 - r, 4))
-        remote(got, got, ogc_s.at[r], ogc_r.at[r], core).wait_recv()
+    remote(og_slot(core_slot), og_slot(core_slot), ogc_s.at[8], ogc_r.at[8], core).wait_recv()
+    for i in range(8):
+        got = og_half(far_slot, quarter((0, 0, 1, 1, 3, 3, 2, 2)[i]), i % 2)
+        remote(got, got, ogc_s.at[i], ogc_r.at[i], core).wait_recv()
 
     @pl.loop(0, 4)
     def _(k):
@@ -220,9 +286,8 @@
                 remote(part.at[r, k], rs.at[r - 1, k], rs_s.at[r - 1, k], rs_r.at[r - 1, k],
                        device(to_x, yl, c, z, yh)).start()
 
-    for i in range(4):
-        there = w_all.at[pl.ds(i * blk, blk)]
-        remote(there, there, w_s.at[0], w_r.at[i], side).wait_recv()
+    for i in (1, 2, 4, 5):
+        wx_wait(i)
     my_rows = pl.ds(mult(mine * rows, rows), rows)
     for r in range(1, 4):
         to, _, k = peer(r)
@@ -345,7 +410,7 @@
             pltpu.VMEM((blk, cols), F32),
             pltpu.VMEM((blk, cols), F32),
             pltpu.VMEM((blk, cols), F32),
-            pltpu.VMEM((blk, cols), BF16),
+            pltpu.VMEM((4, blk, cols // 4), BF16),
             pltpu.VMEM((16, 2, blk, sub), BF16),
             pltpu.VMEM((4 * tok, cols), BF16),
             pltpu.VMEM((ff, tok), BF16),
@@ -360,11 +425,12 @@
             pltpu.VMEM((tok, ff), BF16),
             dma((6,)),
             dma((4,)),
-            dma(()), dma(()),
-            dma((3,)), dma((3,)),
-            dma((5,)), dma((5,)),
+            dma((2,)), dma((2,)),
+            dma((6,)), dma((6,)),
+            dma((9,)), dma((9,)),
             dma((3,)), dma((3,)),
             dma((4,)), dma((4,)),
+            dma((6,)), dma((6,)),
             dma((16,)), dma(()),
             dma((3,)), dma((3,)),
             dma((3,)), dma((3,)),

time: 270 us -> 173 us (0.64)
  the two profiles are of different devices: /device:TPU:7 before, /device:TPU:61 now
where the time goes in v2:
time: 173 us
  Pallas kernels  164 us (95%)
  other arithmetic  5.46 us (3%)
  local copies, waits for them, and re-layouts  2.91 us (2%)
    pallas_call x1, Pallas kernels, body(): pl.pallas_call(kernel, out_shape=(jax.ShapeDtypeStruct((tok, ff), BF16),...  164 us
    sub x1, other arithmetic, adamw(): weight - learn_rate * (first_hat / (jnp.sqrt(second_hat) + epsilon) + dec...  5.46 us

profile of v2, /device:TPU:61, one launch (start us, length us, event | category | flops | bytes accessed | tf_op | source)
XLA Modules:
  0.0 173.0 jit_solution(11498535371397598037)
XLA Ops:
  0.6 163.9 %step.1 = (bf16[384,1792]{1,0:T(8,128)(2,1)}, bf16[384,1792]{1,0:T(8,128)(2,1)}, bf16[1792,256]{1,0:T(8,128)(2,1)}, bf16[2,1792,256]{2,1,0:T(8,128)(2,1)}, bf16[1792,256]{1,0:T(8,128)(2,1)}) custom-call(bf16[384,1792]{1,0:T(8,128)(2,1)} %gate_hbm.1, bf16[384,1792]{1,0:T(8,128)(2,1)} %up_hbm.1, bf16[384,4096]{1,0:T(8,128)(2,1)} %og_hbm.1, f32[112,4096]{1,0:T(8,128)} %w_hbm.1, ...), custom_call_target="tpu_custom_call" | custom-call | flops 11274289152 | bytes 8257536 | tf_op jit(solution)/shard_map/step/pallas_call | solution.py:396
  164.6 0.0 copy-start.1
  164.6 5.5 %convert_subtract_fusion = (f32[1792,256]{1,0:T(8,128)}, f32[1792,256]{1,0:T(8,128)}, f32[1792,256]{1,0:T(8,128)}) fusion(bf16[1792,256]{1,0:T(8,128)(2,1)} %get-tuple-element.10, bf16[1792,256]{1,0:T(8,128)(2,1)} %get-tuple-element.12, bf16[2,1792,256]{2,1,0:T(8,128)(2,1)} %get-tuple-element.11), kind=kLoop, calls=%fused_computation.2 | loop fusion | flops 7798784 | bytes 9175040 | tf_op jit(solution)/shard_map/sub | solution.py:26
  170.1 0.0 copy-start
  170.1 0.0 copy-done.1
  170.1 1.1 copy.13
  171.1 0.8 copy-done
  171.9 1.1 copy.14
Async XLA Ops:
  164.6 5.5 %copy-start.1 = (bf16[384,1792]{1,0:T(8,128)(2,1)S(1)}, bf16[384,1792]{1,0:T(8,128)(2,1)}, u32[]{:S(2)}) copy-start(bf16[384,1792]{1,0:T(8,128)(2,1)} %get-tuple-element.26) | copy-start | bytes 4128772
  170.1 1.8 %copy-start = (bf16[384,1792]{1,0:T(8,128)(2,1)S(1)}, bf16[384,1792]{1,0:T(8,128)(2,1)}, u32[]{:S(2)}) copy-start(bf16[384,1792]{1,0:T(8,128)(2,1)} %get-tuple-element.27) | copy-start | bytes 4128772

commit v3 on v2

--- a/solution.py
+++ b/solution.py
@@ -56,7 +56,7 @@
     sub = cols // 16
     rows = 4 * blk
     tq = tok // 4
-    mine = 2 * c + yl
+    mine = 2 * yl + c
     diag = p == q
     diag_i = jnp.where(diag, 1, 0)
 
@@ -66,7 +66,7 @@
     def peer(r):
         pyl = lax.rem(yl + r % 2, 2)
         pc = lax.rem(c + r // 2, 2)
-        return device(x, pyl, pc, z, yh), 2 * pc + pyl, 2 * pyl + pc
+        return device(x, pyl, pc, z, yh), 2 * pyl + pc
 
     def across(r):
         return lax.rem(x + r, 4)
@@ -133,16 +133,16 @@
     def og_slot(slot):
         return og_all.at[pl.ds(mult(slot * tok, tok), tok)]
 
-    side, side_slot, _ = peer(1)
-    core, core_slot, _ = peer(2)
-    _, far_slot, _ = peer(3)
+    side, side_slot = peer(1)
+    core, core_slot = peer(2)
+    _, far_slot = peer(3)
     for i in range(2):
         mine_half = og_half(mine, z, i)
         go(mine_half, mine_half, ogy_s.at[i], ogy_r.at[i], side)
 
     block = 2 * lax.rem(z, 2) + yh
-    w_yl = z // 2
-    self_w = jnp.logical_and(diag, w_yl == yl)
+    w_core = z // 2
+    self_w = jnp.logical_and(diag, jnp.logical_and(c == yl, w_core == c))
 
     def w_cols(at_x):
         return pl.ds(mult(at_x * 4 * sub, 128), 4 * sub)
@@ -152,8 +152,8 @@
 
     for r in (1, 3, 2):
         go(wb.at[across(r)], w_place(across(r)), w_s.at[r], w_r.at[block],
-           device(across(r), w_yl, c, x, yl))
-    w_home = remote(wb.at[x], w_place(x), w_s.at[0], w_r.at[block], device(x, w_yl, c, x, yl))
+           device(across(r), c, w_core, x, yl))
+    w_home = remote(wb.at[x], w_place(x), w_s.at[0], w_r.at[block], device(x, c, w_core, x, yl))
 
     @pl.when(self_w)
     def _():
@@ -180,10 +180,15 @@
     def _():
         remote(mvb.at[d], mv_dst, mv_s.at[0], mv_r, (d, p)).start()
 
-    @pl.loop(1, 16)
-    def _(r):
-        n = lax.rem(d + r, 16)
-        remote(mvb.at[n], mv_dst, mv_s.at[r], mv_r, (n, p)).start()
+    @pl.loop(0, 4)
+    def _(k):
+        for r in (1, 3, 2, 0):
+            n = across(r) * 4 + lax.rem(mine + k, 4)
+            i = k * 4 + r
+
+            @pl.when(i > 0)
+            def _():
+                remote(mvb.at[n], mv_dst, mv_s.at[i], mv_r, (n, p)).start()
 
     loads[2].wait()
     loads[3].wait()
@@ -198,7 +203,7 @@
 
     my_cols = pl.ds(mult(mine * tok, 128), tok)
     for r in range(1, 4):
-        to, slot, _ = peer(r)
+        to, slot = peer(r)
         go(h_own.at[pl.ds(mult(slot * rows, rows), rows)], h_all.at[:, my_cols],
            h_s.at[r - 1], h_r.at[r - 1], to)
     h_all[:, my_cols] = h_own[pl.ds(mult(mine * rows, rows), rows), :]
@@ -266,7 +271,7 @@
         z_wait(i)
 
     for r in range(1, 4):
-        _, slot, _ = peer(r)
+        _, slot = peer(r)
         there = h_all.at[:, pl.ds(mult(slot * tok, 128), tok)]
         remote(there, there, h_s.at[r - 1], h_r.at[r - 1], side).wait_recv()
     remote(og_slot(core_slot), og_slot(core_slot), ogc_s.at[8], ogc_r.at[8], core).wait_recv()
@@ -290,7 +295,7 @@
         wx_wait(i)
     my_rows = pl.ds(mult(mine * rows, rows), rows)
     for r in range(1, 4):
-        to, _, k = peer(r)
+        to, k = peer(r)
         go(w_all.at[:, pl.ds(mult((x * 4 + k) * sub, 128), sub)], wt_out.at[my_rows],
            wt_s.at[r - 1], wt_r.at[r - 1], to)
     wt_own = pltpu.make_async_copy(
@@ -308,7 +313,7 @@
         ).astype(BF16)
 
     for r in range(1, 4):
-        to, slot, _ = peer(r)
+        to, slot = peer(r)
         go(hg.at[:, pl.ds(mult(slot * tok, 128), tok)], hg_all.at[my_rows],
            hg_s.at[r - 1], hg_r.at[r - 1], to)
     hg_all[my_rows, :] = hg[:, my_cols]
@@ -336,7 +341,7 @@
 
     def finish_grads():
         for r in range(1, 4):
-            _, slot, _ = peer(r)
+            _, slot = peer(r)
             there = hg_all.at[pl.ds(mult(slot * rows, rows), rows)]
             remote(there, there, hg_s.at[r - 1], hg_r.at[r - 1], side).wait_recv()
 
@@ -379,7 +384,7 @@
     wt_own.wait()
     pltpu.make_async_copy(summed.at[0], grad_out.at[my_rows], store_sem.at[1]).wait()
     for r in range(1, 4):
-        _, slot, _ = peer(r)
+        _, slot = peer(r)
         there = pl.ds(mult(slot * rows, rows), rows)
         remote(wt_out.at[there], wt_out.at[there], wt_s.at[r - 1], wt_r.at[r - 1], side).wait_recv()
         remote(summed.at[r], grad_out.at[there], g_s.at[r], g_r.at[r], side).wait()

time: 173 us -> 145 us (0.84)
  the two profiles are of different devices: /device:TPU:61 before, /device:TPU:1 now
where the time goes in v3:
time: 145 us
  Pallas kernels  136 us (94%)
  other arithmetic  5.46 us (4%)
  local copies, waits for them, and re-layouts  2.91 us (2%)
    pallas_call x1, Pallas kernels, body(): pl.pallas_call(kernel, out_shape=(jax.ShapeDtypeStruct((tok, ff), BF16),...  136 us
    sub x1, other arithmetic, adamw(): weight - learn_rate * (first_hat / (jnp.sqrt(second_hat) + epsilon) + dec...  5.46 us
    unnamed x6, local copies, waits for them, and re-layouts  2.91 us

profile of v3, /device:TPU:1, one launch (start us, length us, event | category | flops | bytes accessed | tf_op | source)
XLA Modules:
  0.0 145.0 jit_solution(3273140104946183037)
XLA Ops:
  0.6 136.0 %step.1 = (bf16[384,1792]{1,0:T(8,128)(2,1)}, bf16[384,1792]{1,0:T(8,128)(2,1)}, bf16[1792,256]{1,0:T(8,128)(2,1)}, bf16[2,1792,256]{2,1,0:T(8,128)(2,1)}, bf16[1792,256]{1,0:T(8,128)(2,1)}) custom-call(bf16[384,1792]{1,0:T(8,128)(2,1)} %gate_hbm.1, bf16[384,1792]{1,0:T(8,128)(2,1)} %up_hbm.1, bf16[384,4096]{1,0:T(8,128)(2,1)} %og_hbm.1, f32[112,4096]{1,0:T(8,128)} %w_hbm.1, ...), custom_call_target="tpu_custom_call" | custom-call | flops 11274289152 | bytes 8257536 | tf_op jit(solution)/shard_map/step/pallas_call | solution.py:401
  136.6 0.0 copy-start.1
  136.7 5.5 %convert_subtract_fusion = (f32[1792,256]{1,0:T(8,128)}, f32[1792,256]{1,0:T(8,128)}, f32[1792,256]{1,0:T(8,128)}) fusion(bf16[1792,256]{1,0:T(8,128)(2,1)} %get-tuple-element.10, bf16[1792,256]{1,0:T(8,128)(2,1)} %get-tuple-element.12, bf16[2,1792,256]{2,1,0:T(8,128)(2,1)} %get-tuple-element.11), kind=kLoop, calls=%fused_computation.2 | loop fusion | flops 7798784 | bytes 9175040 | tf_op jit(solution)/shard_map/sub | solution.py:26
  142.1 0.0 copy-start
  142.1 0.0 copy-done.1
  142.1 1.1 copy.13
  143.2 0.8 copy-done
  143.9 1.1 copy.14
Async XLA Ops:
  136.6 5.5 %copy-start.1 = (bf16[384,1792]{1,0:T(8,128)(2,1)S(1)}, bf16[384,1792]{1,0:T(8,128)(2,1)}, u32[]{:S(2)}) copy-start(bf16[384,1792]{1,0:T(8,128)(2,1)} %get-tuple-element.26) | copy-start | bytes 4128772
  142.1 1.8 %copy-start = (bf16[384,1792]{1,0:T(8,128)(2,1)S(1)}, bf16[384,1792]{1,0:T(8,128)(2,1)}, u32[]{:S(2)}) copy-start(bf16[384,1792]{1,0:T(8,128)(2,1)} %get-tuple-element.27) | copy-start | bytes 4128772

commit v4 on v3

--- a/solution.py
+++ b/solution.py
@@ -37,10 +37,10 @@
     gate_hbm, up_hbm, og_hbm, w_hbm, m_hbm, v_hbm,
     gg_hbm, gu_hbm, grad_out, mv_out, wt_out,
     gate, up, w32, m32, v32, wb, mvb, og_all, h_own, h_all, w_all,
-    part, rs, summed, hg, hg_all, gg, gu,
+    part, rs, mid, rs2, summed, hg, hg_all, gg, gu,
     load_sem, store_sem,
     ogy_s, ogy_r, ogz_s, ogz_r, ogc_s, ogc_r, h_s, h_r, w_s, w_r, wx_s, wx_r, mv_s, mv_r,
-    hg_s, hg_r, wt_s, wt_r, rs_s, rs_r, g_s, g_r,
+    hg_s, hg_r, wt_s, wt_r, rs_s, rs_r, rs2_s, rs2_r, g_s, g_r,
 ):
     d = lax.axis_index("dp")
     q = lax.axis_index("tensor")
@@ -279,17 +279,28 @@
         got = og_half(far_slot, quarter((0, 0, 1, 1, 3, 3, 2, 2)[i]), i % 2)
         remote(got, got, ogc_s.at[i], ogc_r.at[i], core).wait_recv()
 
+    near = x + 1 - 2 * lax.rem(x, 2)
+    far = 3 - x
+    opposite = 3 - near
+
+    def at_x(other):
+        return device(other, yl, c, z, yh)
+
     @pl.loop(0, 4)
     def _(k):
-        for r in (1, 3, 2, 0):
-            to_x = across(r)
+        odd = lax.rem(k, 2)
+        first = jnp.where(odd == 1, far, near)
+        second = jnp.where(odd == 1, near, far)
+        for i, to_x in enumerate((first, opposite, x, second)):
             at = pl.ds(mult((to_x * 4 + k) * sub, 128), sub)
-            part[r, k] = jnp.dot(
-                h_all[...], og_all[:, at], preferred_element_type=F32
-            ).astype(BF16)
-            if r:
-                remote(part.at[r, k], rs.at[r - 1, k], rs_s.at[r - 1, k], rs_r.at[r - 1, k],
-                       device(to_x, yl, c, z, yh)).start()
+            part[k, i] = jnp.dot(h_all[...], og_all[:, at], preferred_element_type=F32).astype(BF16)
+            if i == 1:
+                remote(part.at[k, pl.ds(0, 2)], rs.at[k], rs_s.at[k], rs_r.at[k], at_x(first)).start()
+
+    def middle(k):
+        remote(rs.at[k], rs.at[k], rs_s.at[k], rs_r.at[k], side).wait_recv()
+        mid[k] = (part[k, 3].astype(F32) + rs[k, 1].astype(F32)).astype(BF16)
+        go(mid.at[k], rs2.at[k], rs2_s.at[k], rs2_r.at[k], at_x((far, near)[k % 2]))
 
     for i in (1, 2, 4, 5):
         wx_wait(i)
@@ -318,12 +329,13 @@
            hg_s.at[r - 1], hg_r.at[r - 1], to)
     hg_all[my_rows, :] = hg[:, my_cols]
 
+    for k in range(4):
+        middle(k)
+
     def reduce_chunk(k):
-        for r in range(3):
-            remote(rs.at[r, k], rs.at[r, k], rs_s.at[r, k], rs_r.at[r, k], side).wait_recv()
+        remote(rs2.at[k], rs2.at[k], rs2_s.at[k], rs2_r.at[k], side).wait_recv()
         summed[k] = (
-            part[0, k].astype(F32) + rs[0, k].astype(F32)
-            + (rs[1, k].astype(F32) + rs[2, k].astype(F32))
+            part[k, 2].astype(F32) + rs[k, 0].astype(F32) + rs2[k].astype(F32)
         ).astype(BF16)
         k_yl = k // 2
         k_c = k % 2
@@ -376,9 +388,8 @@
 
     for r in range(1, 16):
         remote(mvb.at[r], mv_dst, mv_s.at[r], mv_r, side).wait_send()
-    for r in range(3):
-        for k in range(4):
-            remote(part.at[r + 1, k], rs.at[r, k], rs_s.at[r, k], rs_r.at[r, k], side).wait_send()
+    for k in range(4):
+        remote(part.at[k, pl.ds(0, 2)], rs.at[k], rs_s.at[k], rs_r.at[k], side).wait_send()
     pltpu.make_async_copy(gg, gg_hbm, store_sem.at[2]).wait()
     pltpu.make_async_copy(gu, gu_hbm, store_sem.at[3]).wait()
     wt_own.wait()
@@ -422,7 +433,9 @@
             pltpu.VMEM((rows, 4 * tok), BF16),
             pltpu.VMEM((rows, cols), BF16),
             pltpu.VMEM((4, 4, rows, sub), BF16),
-            pltpu.VMEM((3, 4, rows, sub), BF16),
+            pltpu.VMEM((4, 2, rows, sub), BF16),
+            pltpu.VMEM((4, rows, sub), BF16),
+            pltpu.VMEM((4, rows, sub), BF16),
             pltpu.VMEM((4, rows, sub), BF16),
             pltpu.VMEM((rows, 4 * tok), BF16),
             pltpu.VMEM((ff, tok), BF16),
@@ -439,7 +452,8 @@
             dma((16,)), dma(()),
             dma((3,)), dma((3,)),
             dma((3,)), dma((3,)),
-            dma((3, 4)), dma((3, 4)),
+            dma((4,)), dma((4,)),
+            dma((4,)), dma((4,)),
             dma((4,)), dma((4,)),
         ],
         compiler_params=pltpu.CompilerParams(

time: 145 us -> 140 us (0.966); the launches traced: 145 us -> 138 us
  Pallas kernels: 136 us -> 129 us
    pallas_call x1, Pallas kernels: 136 us -> 129 us  [body(): pl.pallas_call(kernel, out_shape=(jax.ShapeDtypeStruct((tok, ff), BF16),...]
where the time goes in v4:
time: 140 us; the launch traced here: 138 us
  Pallas kernels  129 us (92%)
  other arithmetic  5.46 us (4%)
  local copies, waits for them, and re-layouts  2.91 us (2%)
    pallas_call x1, Pallas kernels, body(): pl.pallas_call(kernel, out_shape=(jax.ShapeDtypeStruct((tok, ff), BF16),...  129 us
    sub x1, other arithmetic, adamw(): weight - learn_rate * (first_hat / (jnp.sqrt(second_hat) + epsilon) + dec...  5.46 us
    unnamed x6, local copies, waits for them, and re-layouts  2.91 us

profile of v4, /device:TPU:1, one launch (start us, length us, event | category | flops | bytes accessed | tf_op | source)
XLA Modules:
  0.0 138.4 jit_solution(8708467004533179904)
XLA Ops:
  0.6 129.3 %step.1 = (bf16[384,1792]{1,0:T(8,128)(2,1)}, bf16[384,1792]{1,0:T(8,128)(2,1)}, bf16[1792,256]{1,0:T(8,128)(2,1)}, bf16[2,1792,256]{2,1,0:T(8,128)(2,1)}, bf16[1792,256]{1,0:T(8,128)(2,1)}) custom-call(bf16[384,1792]{1,0:T(8,128)(2,1)} %gate_hbm.1, bf16[384,1792]{1,0:T(8,128)(2,1)} %up_hbm.1, bf16[384,4096]{1,0:T(8,128)(2,1)} %og_hbm.1, f32[112,4096]{1,0:T(8,128)} %w_hbm.1, ...), custom_call_target="tpu_custom_call" | custom-call | flops 11274289152 | bytes 8257536 | tf_op jit(solution)/shard_map/step/pallas_call | solution.py:412
  130.0 0.0 copy-start.1
  130.0 5.5 %convert_subtract_fusion = (f32[1792,256]{1,0:T(8,128)}, f32[1792,256]{1,0:T(8,128)}, f32[1792,256]{1,0:T(8,128)}) fusion(bf16[1792,256]{1,0:T(8,128)(2,1)} %get-tuple-element.10, bf16[1792,256]{1,0:T(8,128)(2,1)} %get-tuple-element.12, bf16[2,1792,256]{2,1,0:T(8,128)(2,1)} %get-tuple-element.11), kind=kLoop, calls=%fused_computation.2 | loop fusion | flops 7798784 | bytes 9175040 | tf_op jit(solution)/shard_map/sub | solution.py:26
  135.4 0.0 copy-start
  135.4 0.0 copy-done.1
  135.4 1.1 copy.13
  136.5 0.8 copy-done
  137.3 1.1 copy.14
Async XLA Ops:
  130.0 5.5 %copy-start.1 = (bf16[384,1792]{1,0:T(8,128)(2,1)S(1)}, bf16[384,1792]{1,0:T(8,128)(2,1)}, u32[]{:S(2)}) copy-start(bf16[384,1792]{1,0:T(8,128)(2,1)} %get-tuple-element.26) | copy-start | bytes 4128772
  135.4 1.8 %copy-start = (bf16[384,1792]{1,0:T(8,128)(2,1)S(1)}, bf16[384,1792]{1,0:T(8,128)(2,1)}, u32[]{:S(2)}) copy-start(bf16[384,1792]{1,0:T(8,128)(2,1)} %get-tuple-element.27) | copy-start | bytes 4128772

commit v5 on v4

--- a/solution.py
+++ b/solution.py
@@ -265,9 +265,11 @@
     y_wait(1)
     z_wait(0)
     z_wait(3)
+    for i in (1, 2):
+        z_wait(i)
     wx_wait(0)
     wx_wait(3)
-    for i in (1, 2, 4, 5):
+    for i in (4, 5):
         z_wait(i)
 
     for r in range(1, 4):
@@ -371,9 +373,8 @@
         pltpu.make_async_copy(gu, gu_hbm, store_sem.at[3]).start()
 
     for k in range(4):
-        if k == 3:
-            finish_grads()
         reduce_chunk(k)
+    finish_grads()
 
     for copy in sends:
         copy.wait_send()

time: 140 us -> 140 us (level)
  no operation moved by 1% of the time
where the time goes in v5:
time: 140 us; the launch traced here: 138 us
  Pallas kernels  129 us (92%)
  other arithmetic  5.46 us (4%)
  local copies, waits for them, and re-layouts  2.91 us (2%)
    pallas_call x1, Pallas kernels, body(): pl.pallas_call(kernel, out_shape=(jax.ShapeDtypeStruct((tok, ff), BF16),...  129 us
    sub x1, other arithmetic, adamw(): weight - learn_rate * (first_hat / (jnp.sqrt(second_hat) + epsilon) + dec...  5.46 us
    unnamed x6, local copies, waits for them, and re-layouts  2.91 us

profile of v5, /device:TPU:1, one launch (start us, length us, event | category | flops | bytes accessed | tf_op | source)
XLA Modules:
  0.0 138.4 jit_solution(11866651533076782152)
XLA Ops:
  0.6 129.3 %step.1 = (bf16[384,1792]{1,0:T(8,128)(2,1)}, bf16[384,1792]{1,0:T(8,128)(2,1)}, bf16[1792,256]{1,0:T(8,128)(2,1)}, bf16[2,1792,256]{2,1,0:T(8,128)(2,1)}, bf16[1792,256]{1,0:T(8,128)(2,1)}) custom-call(bf16[384,1792]{1,0:T(8,128)(2,1)} %gate_hbm.1, bf16[384,1792]{1,0:T(8,128)(2,1)} %up_hbm.1, bf16[384,4096]{1,0:T(8,128)(2,1)} %og_hbm.1, f32[112,4096]{1,0:T(8,128)} %w_hbm.1, ...), custom_call_target="tpu_custom_call" | custom-call | flops 11274289152 | bytes 8257536 | tf_op jit(solution)/shard_map/step/pallas_call | solution.py:413
  130.0 0.0 copy-start.1
  130.0 5.5 %convert_subtract_fusion = (f32[1792,256]{1,0:T(8,128)}, f32[1792,256]{1,0:T(8,128)}, f32[1792,256]{1,0:T(8,128)}) fusion(bf16[1792,256]{1,0:T(8,128)(2,1)} %get-tuple-element.10, bf16[1792,256]{1,0:T(8,128)(2,1)} %get-tuple-element.12, bf16[2,1792,256]{2,1,0:T(8,128)(2,1)} %get-tuple-element.11), kind=kLoop, calls=%fused_computation.2 | loop fusion | flops 7798784 | bytes 9175040 | tf_op jit(solution)/shard_map/sub | solution.py:26
  135.4 0.0 copy-start
  135.4 0.0 copy-done.1
  135.4 1.1 copy.13
  136.5 0.8 copy-done
  137.3 1.1 copy.14
Async XLA Ops:
  130.0 5.5 %copy-start.1 = (bf16[384,1792]{1,0:T(8,128)(2,1)S(1)}, bf16[384,1792]{1,0:T(8,128)(2,1)}, u32[]{:S(2)}) copy-start(bf16[384,1792]{1,0:T(8,128)(2,1)} %get-tuple-element.26) | copy-start | bytes 4128772
  135.4 1.8 %copy-start = (bf16[384,1792]{1,0:T(8,128)(2,1)S(1)}, bf16[384,1792]{1,0:T(8,128)(2,1)}, u32[]{:S(2)}) copy-start(bf16[384,1792]{1,0:T(8,128)(2,1)} %get-tuple-element.27) | copy-start | bytes 4128772
